TPU v7x, 32 devices: a whole 2x2x4 slice. The times are simulated.
32 devices in a mesh: rep: 4 (over x, core), shard: 8 (over z, y).
Axes of the slice: x: 2, y: 2, z: 4, core: 2. Of those that a mesh axis runs over, the one named last changes fastest.
Arguments:
- tokens: bfloat16 [4, 4096, 1280], P('rep', 'shard'), may hold values from -6 to 6
- segments: int32 [4, 4096], P('rep', 'shard'), may hold values from 0 to 1, as said below
- cotangent: bfloat16 [4, 4096, 1280], P('rep', 'shard'), may hold values from -6 to 6
- gain_one: bfloat16 [1280], P('shard'), may hold values from 0.099609375 to 1.8984375
- qkv_weight: bfloat16 [1280, 3840], P('shard'), may hold values from -0.15625 to 0.15625
- query_scale: float32 [80], replicated, may hold values from 0.5 to 2.5
- out_weight: bfloat16 [1280, 1280], P('shard'), may hold values from -1.25 to 1.25
- gain_two: bfloat16 [1280], P('shard'), may hold values from 0.099609375 to 1.8984375
- up_weight: bfloat16 [1280, 1280], P('shard'), may hold values from -0.15625 to 0.15625
- up_bias: bfloat16 [1280], P('shard'), may hold values from -3 to 3
- down_weight: bfloat16 [1280, 1280], P('shard'), may hold values from -0.15625 to 0.15625
- down_bias: bfloat16 [1280], P('shard'), may hold values from -3 to 3
Outputs:
- output: bfloat16 [4, 4096, 1280], P('rep', 'shard')
- input_grad: bfloat16 [4, 4096, 1280], P('rep', 'shard')
- gain_one_grad: float32 [1280], P('shard')
- qkv_grad: float32 [1280, 3840], P('shard')
- scale_grad: float32 [80], replicated
- out_grad: float32 [1280, 1280], P('shard')
- gain_two_grad: float32 [1280], P('shard')
- up_grad: float32 [1280, 1280], P('shard')
- up_bias_grad: float32 [1280], P('shard')
- down_grad: float32 [1280, 1280], P('shard')
- down_bias_grad: float32 [1280], P('shard')
Inputs may be any that keep to these rules, and one draw needn't show every extreme that they name: `segments`: along each sequence the document numbers start at 0, never fall and each covers one contiguous run of tokens. A sequence holds 2 documents, or one where that is zero; every document but the last holds 1025 to 3071 tokens.
All inputs are finite; a program needn't handle non-finite values.
Results may differ from a plain program's by a relative error of at most 0.019.
Values may be sent and summed in bfloat16 or wider, within the bound.
A program may use at most 320 MiB of HBM per device.

v0:
```python
import math

import jax
import jax.numpy as jnp
from jax import lax
from jax.sharding import PartitionSpec as P

HEAD = 80
WINDOW = 1024


EPS = 1e-06
LOG2E = 1.442695041
MASKED = -1e30
GROUP = 8


def from_behind(value, axis, steps):
    count = lax.axis_size(axis)
    first, last = (max(0, -steps), min(count, count - steps))
    return lax.ppermute(value, axis, [(source, source + steps) for source in range(first, last)])


def rms_scale(state, gain):
    inverse = lax.rsqrt(jnp.mean(state * state, axis=-1, keepdims=True) + EPS)
    return state * inverse * gain


def body(
    tokens,
    segments,
    cotangent,
    gain_one,
    qkv_weight,
    query_scale,
    out_weight,
    gain_two,
    up_weight,
    up_bias,
    down_weight,
    down_bias,
):
    count = tokens.shape[1]
    width = tokens.shape[2]
    reach = WINDOW // count
    block = min(512, count)
    span = WINDOW + block
    heads = width // HEAD
    cols = GROUP * HEAD
    f32 = jnp.float32
    bf16 = jnp.bfloat16
    gain_full_one, qkv_full, out_full = (
        lax.all_gather(gain_one, "shard", axis=0, tiled=True),
        lax.all_gather(qkv_weight, "shard", axis=0, tiled=True),
        lax.all_gather(out_weight, "shard", axis=0, tiled=True),
    )
    gain_full_two, up_full, up_bias_full, down_full, down_bias_full = (
        lax.all_gather(gain_two, "shard", axis=0, tiled=True),
        lax.all_gather(up_weight, "shard", axis=0, tiled=True),
        lax.all_gather(up_bias, "shard", axis=0, tiled=True),
        lax.all_gather(down_weight, "shard", axis=0, tiled=True),
        lax.all_gather(down_bias, "shard", axis=0, tiled=True),
    )
    state = tokens[0].astype(f32)
    own_segments = segments[0]
    normed, norm_pull = jax.vjp(rms_scale, state, gain_full_one.astype(f32))
    acted = normed.astype(bf16)
    mixed = jnp.dot(acted, qkv_full, preferred_element_type=f32)
    query_raw = mixed[:, :width]
    factor = jnp.tile(LOG2E / math.sqrt(HEAD) * jax.nn.softplus(query_scale), heads)
    queries = (query_raw * factor).astype(bf16)
    keys = mixed[:, width : 2 * width].astype(bf16)
    values = mixed[:, 2 * width :].astype(bf16)
    moving = (keys, values, own_segments + 1)
    pieces = [moving]
    for turn in range(reach):
        moving = from_behind((moving[0], moving[1], moving[2]), "shard", 1)
        pieces = [moving] + pieces
    ext_keys = jnp.concatenate([piece[0] for piece in pieces], 0)
    ext_values = jnp.concatenate([piece[1] for piece in pieces], 0)
    ext_segments = jnp.concatenate([piece[2] for piece in pieces], 0) - 1
    rows = lax.broadcasted_iota(jnp.int32, (block, span), 0)
    columns = lax.broadcasted_iota(jnp.int32, (block, span), 1)
    near = (columns > rows) & (columns <= rows + WINDOW)

    def block_mask():
        return near & (own_segments[:, None] == ext_segments[None, :])

    def scores_of(first, column, allowed):
        shaped_query = queries[first : first + block, column : column + cols].reshape(
            block, GROUP, HEAD
        )
        shaped_key = ext_keys[first : first + span, column : column + cols].reshape(
            span, GROUP, HEAD
        )
        raw = jnp.einsum("qhd,khd->hqk", shaped_query, shaped_key, preferred_element_type=f32)
        return jnp.where(allowed[None], raw, MASKED)

    first = 0
    allowed = block_mask()
    parts = []
    block_sums = []
    for column in range(0, width, cols):
        scores = scores_of(first, column, allowed)
        top = jnp.max(scores, axis=-1, keepdims=True)
        expo = jnp.exp(scores - top)
        total = jnp.sum(expo, axis=-1, keepdims=True)
        probs = (expo / total).astype(bf16)
        shaped_value = ext_values[first : first + span, column : column + cols].reshape(
            span, GROUP, HEAD
        )
        mixed_out = jnp.einsum("hqk,khd->qhd", probs, shaped_value, preferred_element_type=f32)
        parts.append(mixed_out.reshape(block, cols))
        block_sums.append(top + jnp.log(total))
    outputs = jnp.concatenate(parts, 1)
    logsums = [block_sums]
    heads_out = outputs.astype(bf16)
    hidden = state + jnp.dot(heads_out, out_full, preferred_element_type=f32)
    normed_two, norm_pull_two = jax.vjp(rms_scale, hidden, gain_full_two.astype(f32))
    inner = normed_two.astype(bf16)
    upper = jnp.dot(inner, up_full, preferred_element_type=f32) + up_bias_full.astype(f32)
    lower_full, silu_pull = jax.vjp(jax.nn.silu, upper)
    lower = lower_full.astype(bf16)
    result = hidden + (
        jnp.dot(lower, down_full, preferred_element_type=f32) + down_bias_full.astype(f32)
    )
    output = result.astype(bf16)[None]
    qkv_full, out_full = (
        lax.all_gather(qkv_weight, "shard", axis=0, tiled=True),
        lax.all_gather(out_weight, "shard", axis=0, tiled=True),
    )
    up_full, down_full = (
        lax.all_gather(up_weight, "shard", axis=0, tiled=True),
        lax.all_gather(down_weight, "shard", axis=0, tiled=True),
    )
    grad_out = cotangent[0].astype(f32)
    grad_low = cotangent[0]
    down_grad = jnp.einsum("tf,td->fd", lower, grad_low, preferred_element_type=f32)
    down_bias_grad = jnp.sum(grad_out, axis=0)
    grad_lower = jnp.einsum("td,fd->tf", grad_low, down_full, preferred_element_type=f32)
    grad_upper = silu_pull(grad_lower)[0].astype(bf16)
    up_grad = jnp.einsum("td,tf->df", inner, grad_upper, preferred_element_type=f32)
    up_bias_grad = jnp.sum(grad_upper.astype(f32), axis=0)
    grad_inner = jnp.einsum("tf,df->td", grad_upper, up_full, preferred_element_type=f32)
    grad_hidden_norm, gain_two_grad = norm_pull_two(grad_inner)
    grad_hidden = grad_out + grad_hidden_norm
    grad_attn = grad_hidden.astype(bf16)
    out_grad = jnp.einsum("tf,td->fd", heads_out, grad_attn, preferred_element_type=f32)
    grad_heads = jnp.einsum("td,fd->tf", grad_attn, out_full, preferred_element_type=f32).astype(
        bf16
    )
    ext_rows = (reach + 1) * count
    grad_keys_ext = jnp.zeros((ext_rows, width), f32)
    grad_values_ext = jnp.zeros((ext_rows, width), f32)
    grad_query_blocks = []
    for index, first in enumerate(range(0, count, block)):
        allowed = block_mask()
        query_parts = []
        key_parts = []
        value_parts = []
        for number, column in enumerate(range(0, width, cols)):
            scores = scores_of(first, column, allowed)
            probs = jnp.exp(scores - logsums[index][number])
            shaped_grad = grad_heads[first : first + block, column : column + cols].reshape(
                block, GROUP, HEAD
            )
            shaped_value = ext_values[first : first + span, column : column + cols].reshape(
                span, GROUP, HEAD
            )
            shaped_key = ext_keys[first : first + span, column : column + cols].reshape(
                span, GROUP, HEAD
            )
            shaped_query = queries[first : first + block, column : column + cols].reshape(
                block, GROUP, HEAD
            )
            grad_probs = jnp.einsum(
                "qhd,khd->hqk", shaped_grad, shaped_value, preferred_element_type=f32
            )
            value_term = jnp.einsum(
                "hqk,qhd->khd", probs.astype(bf16), shaped_grad, preferred_element_type=f32
            )
            value_parts.append(value_term.reshape(span, cols))
            inner_sum = jnp.sum(probs * grad_probs, axis=-1, keepdims=True)
            grad_scores = (probs * (grad_probs - inner_sum)).astype(bf16)
            query_term = jnp.einsum(
                "hqk,khd->qhd", grad_scores, shaped_key, preferred_element_type=f32
            )
            query_parts.append(query_term.reshape(block, cols))
            key_term = jnp.einsum(
                "hqk,qhd->khd", grad_scores, shaped_query, preferred_element_type=f32
            )
            key_parts.append(key_term.reshape(span, cols))
        grad_query_blocks.append(jnp.concatenate(query_parts, 1))
        grad_keys_ext = grad_keys_ext.at[first : first + span].add(jnp.concatenate(key_parts, 1))
        grad_values_ext = grad_values_ext.at[first : first + span].add(
            jnp.concatenate(value_parts, 1)
        )
    carry_keys = grad_keys_ext[:count]
    carry_values = grad_values_ext[:count]
    for turn in range(reach):
        arrived = (
            from_behind(carry_keys.astype(jnp.bfloat16), "shard", -1).astype(carry_keys.dtype),
            from_behind(carry_values.astype(jnp.bfloat16), "shard", -1).astype(carry_values.dtype),
        )
        start = (turn + 1) * count
        carry_keys = arrived[0] + grad_keys_ext[start : start + count]
        carry_values = arrived[1] + grad_values_ext[start : start + count]
    grad_keys = carry_keys.astype(bf16)
    grad_values = carry_values.astype(bf16)
    grad_queries = grad_query_blocks[0]
    grad_query_raw = (grad_queries * factor).astype(bf16)
    scale_part = jnp.sum((grad_queries * query_raw).reshape(count, heads, HEAD), axis=(0, 1))
    scale_term = scale_part * (LOG2E / math.sqrt(HEAD)) * jax.nn.sigmoid(query_scale)
    scale_grad = lax.psum(scale_term, ("rep", "shard"))
    grad_mixed = jnp.concatenate([grad_query_raw, grad_keys, grad_values], 1)
    qkv_grad = jnp.einsum("td,tf->df", acted, grad_mixed, preferred_element_type=f32)
    grad_acted = jnp.einsum("tf,df->td", grad_mixed, qkv_full, preferred_element_type=f32)
    grad_state_norm, gain_one_grad = norm_pull(grad_acted)
    input_grad = (grad_hidden + grad_state_norm).astype(bf16)[None]
    owned = (
        lax.psum_scatter(
            gain_one_grad.astype(jnp.bfloat16), "shard", scatter_dimension=0, tiled=True
        ).astype(jnp.float32),
        lax.psum_scatter(
            qkv_grad.astype(jnp.bfloat16), "shard", scatter_dimension=0, tiled=True
        ).astype(jnp.float32),
        lax.psum_scatter(
            out_grad.astype(jnp.bfloat16), "shard", scatter_dimension=0, tiled=True
        ).astype(jnp.float32),
        lax.psum_scatter(
            gain_two_grad.astype(jnp.bfloat16), "shard", scatter_dimension=0, tiled=True
        ).astype(jnp.float32),
        lax.psum_scatter(
            up_grad.astype(jnp.bfloat16), "shard", scatter_dimension=0, tiled=True
        ).astype(jnp.float32),
        lax.psum_scatter(
            up_bias_grad.astype(jnp.bfloat16), "shard", scatter_dimension=0, tiled=True
        ).astype(jnp.float32),
        lax.psum_scatter(
            down_grad.astype(jnp.bfloat16), "shard", scatter_dimension=0, tiled=True
        ).astype(jnp.float32),
        lax.psum_scatter(
            down_bias_grad.astype(jnp.bfloat16), "shard", scatter_dimension=0, tiled=True
        ).astype(jnp.float32),
    )
    owned = (
        lax.psum(owned[0].astype(jnp.bfloat16), "rep").astype(jnp.float32),
        lax.psum(owned[1].astype(jnp.bfloat16), "rep").astype(jnp.float32),
        lax.psum(owned[2].astype(jnp.bfloat16), "rep").astype(jnp.float32),
        lax.psum(owned[3].astype(jnp.bfloat16), "rep").astype(jnp.float32),
        lax.psum(owned[4].astype(jnp.bfloat16), "rep").astype(jnp.float32),
        lax.psum(owned[5].astype(jnp.bfloat16), "rep").astype(jnp.float32),
        lax.psum(owned[6].astype(jnp.bfloat16), "rep").astype(jnp.float32),
        lax.psum(owned[7].astype(jnp.bfloat16), "rep").astype(jnp.float32),
    )
    return (
        output,
        input_grad,
        owned[0],
        owned[1],
        scale_grad,
        owned[2],
        owned[3],
        owned[4],
        owned[5],
        owned[6],
        owned[7],
    )


def solution(mesh):
    return jax.shard_map(
        body,
        mesh=mesh,
        in_specs=(
            P("rep", "shard", None),
            P("rep", "shard"),
            P("rep", "shard", None),
            P("shard"),
            P("shard", None),
            P(),
            P("shard", None),
            P("shard"),
            P("shard", None),
            P("shard"),
            P("shard", None),
            P("shard"),
        ),
        out_specs=(
            P("rep", "shard", None),
            P("rep", "shard", None),
            P("shard"),
            P("shard", None),
            P(),
            P("shard", None),
            P("shard"),
            P("shard", None),
            P("shard"),
            P("shard", None),
            P("shard"),
        ),
        check_vma=False,
    )
```

profile of v0, /device:TPU:0, one launch (start us, length us, event | category | flops | bytes accessed | tf_op | source)
XLA Modules:
  0.0 1047.3 jit_solution(2601573466953757994)
XLA Ops:
  14.0 40.1 %all-reduce.9 = (bf16[1280]{0:T(1024)(128)(2,1)S(1)}, bf16[1280]{0:T(1024)(128)(2,1)S(1)}, bf16[1280]{0:T(1024)(128)(2,1)S(1)}) all-reduce(bf16[1280]{0:T(1024)(128)(2,1)S(1)} %dynamic-update-slice.4, bf16[1280]{0:T(1024)(128)(2,1)S(1)} %dynamic-update-slice.6, ...), channel_id=1, replica_groups=mesh['rep'=4,'shard'=8] {'shard'}, use_global_device_ids=true, to_apply=%add | all-reduce | flops 3840 | bytes 15360
  55.0 101.1 %all-gather.5.cloned.1.call-done = bf16[1280,3840]{1,0:T(8,128)(2,1)} async-done(((bf16[160,3840]{1,0:T(8,128)(2,1)}), bf16[1280,3840]{1,0:T(8,128)(2,1)}) %all-gather.5.cloned.1.call-update) | async-done | bytes 9830416 | tf_op jit(solution)/shard_map/all_gather | solution.py:54
  172.8 30.3 %collective-permute-done.2 = s32[512]{0:T(512)S(1)} collective-permute-done((s32[512]{0:T(512)S(1)}, s32[512]{0:T(512)S(1)}, u32[]{:S(2)}, u32[]{:S(2)}) %collective-permute-start.2) | collective-permute-done | bytes 2080 | tf_op jit(solution)/shard_map/ppermute | solution.py:21
  203.1 20.0 %collective-permute-start.3 = (s32[512]{0:T(512)S(1)}, s32[512]{0:T(512)S(1)}, u32[]{:S(2)}, u32[]{:S(2)}) collective-permute-start(s32[512]{0:T(512)S(1)} %collective-permute-done.2), channel_id=1, source_target_pairs={{0,1},{1,2},{2,3},{3,4},{4,5},{5,6},{6,7},{8,9},{9,10},{10,11},{11... | collective-permute-start | bytes 6152 | tf_op jit(solution)/shard_map/ppermute | solution.py:21
  229.7 13.2 %collective-permute-start.5 = (bf16[512,1280]{1,0:T(8,128)(2,1)}, bf16[512,1280]{1,0:T(8,128)(2,1)}, u32[]{:S(2)}, u32[]{:S(2)}) collective-permute-start(bf16[512,1280]{1,0:T(8,128)(2,1)} %collective-permute-done.4), channel_id=1, source_target_pairs={{0,1},{1,2},{2,3},{3,4},{4,5},{5,6},{6,7},{8,9},{9,10},{10,11},{11... | collective-permute-start | bytes 3932168 | tf_op jit(solution)/shard_map/ppermute | solution.py:21
  245.9 16.2 %collective-permute-done = bf16[512,1280]{1,0:T(8,128)(2,1)} collective-permute-done((bf16[512,1280]{1,0:T(8,128)(2,1)S(1)}, bf16[512,1280]{1,0:T(8,128)(2,1)}, u32[]{:S(2)}, u32[]{:S(2)}) %collective-permute-start) | collective-permute-done | bytes 1310752 | tf_op jit(solution)/shard_map/ppermute | solution.py:21
  262.1 24.7 %collective-permute-start.1 = (bf16[512,1280]{1,0:T(8,128)(2,1)}, bf16[512,1280]{1,0:T(8,128)(2,1)}, u32[]{:S(2)}, u32[]{:S(2)}) collective-permute-start(bf16[512,1280]{1,0:T(8,128)(2,1)} %collective-permute-done), channel_id=1, source_target_pairs={{0,1},{1,2},{2,3},{3,4},{4,5},{5,6},{6,7},{8,9},{9,10},{10,11},{11... | collective-permute-start | bytes 3932168 | tf_op jit(solution)/shard_map/ppermute | solution.py:21
  307.5 25.7 %collective-permute-done.1 = bf16[512,1280]{1,0:T(8,128)(2,1)} collective-permute-done((bf16[512,1280]{1,0:T(8,128)(2,1)}, bf16[512,1280]{1,0:T(8,128)(2,1)}, u32[]{:S(2)}, u32[]{:S(2)}) %collective-permute-start.1) | collective-permute-done | bytes 1310752 | tf_op jit(solution)/shard_map/ppermute | solution.py:21
  346.2 12.2 %fusion.71 = (f32[8,512]{1,0:T(8,128)S(1)}, f32[8,512,1536]{2,1,0:T(8,128)}) fusion(bf16[512,8,80]{0,2,1:T(8,128)(2,1)} %bitcast.104, bf16[1536,8,80]{0,2,1:T(8,128)(2,1)S(1)} %bitcast.94, pred[512,1536]{1,0:T(8,128)(4,1)S(1)} %fusion.14), kind=kOutput, calls=%fused_computation.130 | convolution fusion | flops 1019211776 | bytes 28590080 | tf_op jit(solution)/shard_map/qhd,khd->hqk/dot_general | solution.py:96
  391.6 11.5 %fusion = f32[8,512]{1,0:T(8,128)S(1)} fusion(f32[8,512,1536]{2,1,0:T(8,128)} %get-tuple-element.90, f32[8,512]{1,0:T(8,128)S(1)} %get-tuple-element.89), kind=kLoop, calls=%fused_computation.10 | loop fusion | flops 12578816 | bytes 25198592 | tf_op jit(solution)/shard_map/reduce_sum | solution.py:107
  455.8 12.3 %fusion.4 = f32[8,80,1536]{2,1,0:T(8,128)} fusion(bf16[512,8,80]{0,2,1:T(8,128)(2,1)S(1)} %bitcast.110, f32[8,512,1536]{2,1,0:T(8,128)} %get-tuple-element.88, f32[8,512]{1,0:T(8,128)S(1)} %log_add_fusion), kind=kOutput, calls=%fused_computation.17 | convolution fusion | flops 1019215872 | bytes 29769728 | tf_op jit(solution)/shard_map/hqk,qhd->khd/dot_general | solution.py:179
  473.6 12.3 %fusion.6 = f32[8,80,1536]{2,1,0:T(8,128)} fusion(bf16[512,8,80]{0,2,1:T(8,128)(2,1)S(1)} %bitcast.112, f32[8,512,1536]{2,1,0:T(8,128)} %get-tuple-element.90, f32[8,512]{1,0:T(8,128)S(1)} %log_add_fusion.1), kind=kOutput, calls=%fused_computation.18 | convolution fusion | flops 1019215872 | bytes 29769728 | tf_op jit(solution)/shard_map/hqk,qhd->khd/dot_general | solution.py:179
  499.6 17.1 %multiply_reduce_fusion.1 = (f32[8,512]{1,0:T(8,128)S(1)}, f32[8,512,1536]{2,1,0:T(8,128)}) fusion(f32[8,512,1536]{2,1,0:T(8,128)} %get-tuple-element.90, f32[8,512]{1,0:T(8,128)S(1)} %log_add_fusion.1, bf16[512,8,80]{0,2,1:T(8,128)(2,1)S(1)} %bitcast.113, bf16[1536,8,80]{0,2,1:T(8,128)(2,1)} %bitcast.108), kind=kOutput, calls=%fused_computation.4 | convolution fusion | flops 1025503232 | bytes 52985856 | tf_op jit(solution)/shard_map/qhd,khd->hqk/dot_general | solution.py:176
  516.7 15.8 %multiply_reduce_fusion = (f32[8,512]{1,0:T(8,128)S(1)}, f32[8,512,1536]{2,1,0:T(8,128)}) fusion(f32[8,512,1536]{2,1,0:T(8,128)} %get-tuple-element.88, f32[8,512]{1,0:T(8,128)S(1)} %log_add_fusion, bf16[512,8,80]{0,2,1:T(8,128)(2,1)S(1)} %bitcast.111, bf16[1536,8,80]{0,2,1:T(8,128)(2,1)S(1)} %bitcast.107), kind=kOutput, calls=%fused_computation.1 | convolution fusion | flops 1025503232 | bytes 52985856 | tf_op jit(solution)/shard_map/qhd,khd->hqk/dot_general | solution.py:176
  533.1 23.3 %multiply_convert_fusion.1 = bf16[8,512,1536]{2,1,0:T(8,128)(2,1)} fusion(f32[8,512,1536]{2,1,0:T(8,128)} %get-tuple-element.97, f32[8,512,1536]{2,1,0:T(8,128)} %get-tuple-element.90, f32[8,512]{1,0:T(8,128)S(1)} %get-tuple-element.96, f32[8,512]{1,0:T(8,128)S(1)} %log_add_fusion.1), kind=kLoop, calls=%fused_computation.3 | loop fusion | flops 25165824 | bytes 62947328 | tf_op jit(solution)/shard_map/convert_element_type | solution.py:184
  560.9 14.9 %multiply_convert_fusion = bf16[8,512,1536]{2,1,0:T(8,128)(2,1)} fusion(f32[8,512,1536]{2,1,0:T(8,128)} %get-tuple-element.95, f32[8,512,1536]{2,1,0:T(8,128)S(1)} %bitcast.93, f32[8,512]{1,0:T(8,128)S(1)} %get-tuple-element.94, f32[8,512]{1,0:T(8,128)S(1)} %log_add_fusion), kind=kLoop, calls=%fused_computation | loop fusion | flops 25165824 | bytes 62947328 | tf_op jit(solution)/shard_map/convert_element_type | solution.py:184
  618.8 64.7 %collective-permute-done.6 = bf16[512,1280]{1,0:T(8,128)(2,1)} collective-permute-done((bf16[512,1280]{1,0:T(8,128)(2,1)}, bf16[512,1280]{1,0:T(8,128)(2,1)}, u32[]{:S(2)}, u32[]{:S(2)}) %collective-permute-start.6) | collective-permute-done | bytes 1310752 | tf_op jit(solution)/shard_map/ppermute | solution.py:21
  701.3 16.6 %collective-permute-done.9 = bf16[512,1280]{1,0:T(8,128)(2,1)} collective-permute-done((bf16[512,1280]{1,0:T(8,128)(2,1)}, bf16[512,1280]{1,0:T(8,128)(2,1)}, u32[]{:S(2)}, u32[]{:S(2)}) %collective-permute-start.9) | collective-permute-done | bytes 1310752 | tf_op jit(solution)/shard_map/ppermute | solution.py:21
  720.0 19.5 %collective-permute-done.7 = bf16[512,1280]{1,0:T(8,128)(2,1)} collective-permute-done((bf16[512,1280]{1,0:T(8,128)(2,1)}, bf16[512,1280]{1,0:T(8,128)(2,1)}, u32[]{:S(2)}, u32[]{:S(2)}) %collective-permute-start.7) | collective-permute-done | bytes 1310752 | tf_op jit(solution)/shard_map/ppermute | solution.py:21
  753.5 65.2 %psum.65 = f32[80]{0:T(128)} all-reduce(f32[80]{0:T(128)S(1)} %divide_multiply_fusion), channel_id=1, replica_groups=mesh['rep'=4,'shard'=8] {'rep','shard'}, use_global_device_ids=true, to_apply=%region_17.18 | all-reduce | flops 80 | bytes 640 | tf_op jit(solution)/shard_map/psum | solution.py:214
  818.7 11.5 %fusion.20 = (bf16[1280]{0:T(1024)(128)(2,1)S(1)}, f32[512]{0:T(512)S(1)}, f32[512,1280]{1,0:T(8,128)}) fusion(bf16[1,512,1280]{2,1,0:T(8,128)(2,1)} %param.20, f32[512]{0:T(512)S(1)} %copy-done.45, f32[1280]{0:T(1024)S(1)} %copy-done.40, bf16[1280,3840]{1,0:T(8,128)(2,1)} %all-gather.5.cloned.1.call-done, bf16[512,1280]{1,0:T(8,128)(2,1)} %copy-done.32, ...), kind=kOutput, calls=%fused_computation.58 | convolution fusion | flops 5049547264 | bytes 17706496 | tf_op jit(solution)/shard_map/tf,df->td/dot_general | solution.py:217
  830.2 38.7 %all-reduce.8 = (bf16[1280]{0:T(1024)(128)(2,1)S(1)}, bf16[1280]{0:T(1024)(128)(2,1)S(1)}, bf16[1280]{0:T(1024)(128)(2,1)S(1)}, bf16[1280]{0:T(1024)(128)(2,1)S(1)}, bf16[1280]{0:T(1024)(128)(2,1)S(1)}) all-reduce(bf16[1280]{0:T(1024)(128)(2,1)S(1)} %dynamic-update-slice.7, ...), channel_id=1, replica_groups=mesh['rep'=4,'shard'=8] {'shard'}, use_global_device_ids=true, to_apply=%add.3 | all-reduce | flops 6400 | bytes 25600
  877.8 96.5 %reduce-scatter.5.cloned.1.call-done = bf16[160,3840]{1,0:T(8,128)(2,1)} async-done(((bf16[1280,3840]{1,0:T(8,128)(2,1)}), bf16[160,3840]{1,0:T(8,128)(2,1)}) %reduce-scatter.5.cloned.1.call-update) | async-done | bytes 1228816 | tf_op jit(solution)/shard_map/reduce_scatter | solution.py:224
  983.4 50.5 %all-reduce.14.cloned.1.call-done = (bf16[160,3840]{1,0:T(8,128)(2,1)}, bf16[160,1280]{1,0:T(8,128)(2,1)}, bf16[160,1280]{1,0:T(8,128)(2,1)}, bf16[160,1280]{1,0:T(8,128)(2,1)}) async-done(((bf16[160,3840]{1,0:T(8,128)(2,1)}, bf16[160,1280]{1,0:T(8,128)(2,1)}, bf16[160,1280]{1,0:T(8,128)(2,1)}, bf16[160,1280]{1,0:T(8,128)(2,1)}), (bf16[160,3840]{1,0:T(8,128)(2,1)}, bf16[160,1280]{1,0:T(8,128)(2,1)}, ...) | async-done | bytes 2457616 | tf_op jit(solution)/shard_map/psum | solution.py:248
  (257 shorter events, 277.1 us)
Async XLA Ops:
  7.2 149.0 %all-gather.5.cloned.1.call-start = ((), (), s32[]{:S(2)}) async-start(), calls=%async_computation.4 | async-start | bytes 11059200 | tf_op jit(solution)/shard_map/all_gather | solution.py:54
  7.9 406.2 %all-gather.7.cloned.1.call-start = ((), (), s32[]{:S(2)}) async-start(), calls=%async_computation.5 | async-start | bytes 3686400 | tf_op jit(solution)/shard_map/all_gather | solution.py:55
  8.7 411.1 %all-gather.9.cloned.1.call-start = ((), (), s32[]{:S(2)}) async-start(), calls=%async_computation.6 | async-start | bytes 3686400 | tf_op jit(solution)/shard_map/all_gather | solution.py:59
  9.4 416.6 %all-gather.11.cloned.1.call-start = ((), (), s32[]{:S(2)}) async-start(), calls=%async_computation.7 | async-start | bytes 3686400 | tf_op jit(solution)/shard_map/all_gather | solution.py:61
  54.1 113.4 %copy-start.39 = (f32[1280]{0:T(1024)}, f32[1280]{0:T(1024)S(1)}, u32[]{:S(2)}) copy-start(f32[1280]{0:T(1024)S(1)} %convert_element_type.161) | copy-start | bytes 15364
  55.0 112.5 %copy-start.44 = (f32[512]{0:T(512)}, f32[512]{0:T(512)S(1)}, u32[]{:S(2)}) copy-start(f32[512]{0:T(512)S(1)} %fusion.57) | copy-start | bytes 6148
  167.7 120.0 %copy-start.26 = (bf16[512,1280]{1,0:T(8,128)(2,1)}, bf16[512,1280]{1,0:T(8,128)(2,1)S(1)}, u32[]{:S(2)}) copy-start(bf16[512,1280]{1,0:T(8,128)(2,1)S(1)} %get-tuple-element.76) | copy-start | bytes 3932164
  167.8 61.9 %collective-permute-start.4 = (bf16[512,1280]{1,0:T(8,128)(2,1)S(1)}, bf16[512,1280]{1,0:T(8,128)(2,1)}, u32[]{:S(2)}, u32[]{:S(2)}) collective-permute-start(bf16[512,1280]{1,0:T(8,128)(2,1)S(1)} %get-tuple-element.75), channel_id=1, source_target_pairs={{0,1},{1,2},{2,3},{3,4},{4,5},{5,6},{6,7},{8,9},{9,10},{10,11},{11... | collective-permute-start | bytes 3932168 | tf_op jit(solution)/shard_map/ppermute | solution.py:21
  171.3 31.8 %collective-permute-start.2 = (s32[512]{0:T(512)S(1)}, s32[512]{0:T(512)S(1)}, u32[]{:S(2)}, u32[]{:S(2)}) collective-permute-start(s32[512]{0:T(512)S(1)} %broadcast_add_fusion.1), channel_id=1, source_target_pairs={{0,1},{1,2},{2,3},{3,4},{4,5},{5,6},{6,7},{8,9},{9,10},{10,11},{11... | collective-permute-start | bytes 6152 | tf_op jit(solution)/shard_map/ppermute | solution.py:21
  172.7 705.0 %reduce-scatter.9.cloned.1.call-start = ((), (), s32[]{:S(2)}) async-start(), calls=%async_computation.10 | async-start | bytes 3686400 | tf_op jit(solution)/shard_map/reduce_scatter | solution.py:233
  203.1 26.5 %collective-permute-start.3 = (s32[512]{0:T(512)S(1)}, s32[512]{0:T(512)S(1)}, u32[]{:S(2)}, u32[]{:S(2)}) collective-permute-start(s32[512]{0:T(512)S(1)} %collective-permute-done.2), channel_id=1, source_target_pairs={{0,1},{1,2},{2,3},{3,4},{4,5},{5,6},{6,7},{8,9},{9,10},{10,11},{11... | collective-permute-start | bytes 6152 | tf_op jit(solution)/shard_map/ppermute | solution.py:21
  223.1 38.9 %collective-permute-start = (bf16[512,1280]{1,0:T(8,128)(2,1)S(1)}, bf16[512,1280]{1,0:T(8,128)(2,1)}, u32[]{:S(2)}, u32[]{:S(2)}) collective-permute-start(bf16[512,1280]{1,0:T(8,128)(2,1)S(1)} %get-tuple-element.76), channel_id=1, source_target_pairs={{0,1},{1,2},{2,3},{3,4},{4,5},{5,6},{6,7},{8,9},{9,10},{10,11},{11... | collective-permute-start | bytes 3932168 | tf_op jit(solution)/shard_map/ppermute | solution.py:21
  229.7 71.6 %collective-permute-start.5 = (bf16[512,1280]{1,0:T(8,128)(2,1)}, bf16[512,1280]{1,0:T(8,128)(2,1)}, u32[]{:S(2)}, u32[]{:S(2)}) collective-permute-start(bf16[512,1280]{1,0:T(8,128)(2,1)} %collective-permute-done.4), channel_id=1, source_target_pairs={{0,1},{1,2},{2,3},{3,4},{4,5},{5,6},{6,7},{8,9},{9,10},{10,11},{11... | collective-permute-start | bytes 3932168 | tf_op jit(solution)/shard_map/ppermute | solution.py:21
  262.1 71.2 %collective-permute-start.1 = (bf16[512,1280]{1,0:T(8,128)(2,1)}, bf16[512,1280]{1,0:T(8,128)(2,1)}, u32[]{:S(2)}, u32[]{:S(2)}) collective-permute-start(bf16[512,1280]{1,0:T(8,128)(2,1)} %collective-permute-done), channel_id=1, source_target_pairs={{0,1},{1,2},{2,3},{3,4},{4,5},{5,6},{6,7},{8,9},{9,10},{10,11},{11... | collective-permute-start | bytes 3932168 | tf_op jit(solution)/shard_map/ppermute | solution.py:21
  289.1 91.9 %copy-start.12 = (bf16[512,640]{0,1:T(8,128)(2,1)}, bf16[512,640]{0,1:T(8,128)(2,1)S(1)}, u32[]{:S(2)}) copy-start(bf16[512,640]{0,1:T(8,128)(2,1)S(1)} %copy.74) | copy-start | bytes 1966084
  436.6 441.2 %reduce-scatter.7.cloned.1.call-start = ((), (), s32[]{:S(2)}) async-start(), calls=%async_computation.9 | async-start | bytes 3686400 | tf_op jit(solution)/shard_map/reduce_scatter | solution.py:227
  455.7 422.1 %reduce-scatter.11.cloned.1.call-start = ((), (), s32[]{:S(2)}) async-start(), calls=%async_computation.11 | async-start | bytes 3686400 | tf_op jit(solution)/shard_map/reduce_scatter | solution.py:239
  494.4 119.3 %collective-permute-start.8 = (bf16[512,1280]{1,0:T(8,128)(2,1)}, bf16[512,1280]{1,0:T(8,128)(2,1)}, u32[]{:S(2)}, u32[]{:S(2)}) collective-permute-start(bf16[512,1280]{1,0:T(8,128)(2,1)} %fusion.33), channel_id=1, source_target_pairs={{1,0},{2,1},{3,2},{4,3},{5,4},{6,5},{7,6},{9,8},{10,9},{11,10},{12... | collective-permute-start | bytes 3932168 | tf_op jit(solution)/shard_map/ppermute | solution.py:21
  532.5 441.8 %reduce-scatter.5.cloned.1.call-start = ((), (), s32[]{:S(2)}) async-start(), calls=%async_computation.8 | async-start | bytes 11059200 | tf_op jit(solution)/shard_map/reduce_scatter | solution.py:224
  603.4 80.2 %collective-permute-start.6 = (bf16[512,1280]{1,0:T(8,128)(2,1)}, bf16[512,1280]{1,0:T(8,128)(2,1)}, u32[]{:S(2)}, u32[]{:S(2)}) collective-permute-start(bf16[512,1280]{1,0:T(8,128)(2,1)} %fusion.38), channel_id=1, source_target_pairs={{1,0},{2,1},{3,2},{4,3},{5,4},{6,5},{7,6},{9,8},{10,9},{11,10},{12... | collective-permute-start | bytes 3932168 | tf_op jit(solution)/shard_map/ppermute | solution.py:21
  617.3 100.6 %collective-permute-start.9 = (bf16[512,1280]{1,0:T(8,128)(2,1)}, bf16[512,1280]{1,0:T(8,128)(2,1)}, u32[]{:S(2)}, u32[]{:S(2)}) collective-permute-start(bf16[512,1280]{1,0:T(8,128)(2,1)} %fusion.31), channel_id=1, source_target_pairs={{1,0},{2,1},{3,2},{4,3},{5,4},{6,5},{7,6},{9,8},{10,9},{11,10},{12... | collective-permute-start | bytes 3932168 | tf_op jit(solution)/shard_map/ppermute | solution.py:21
  686.3 53.3 %collective-permute-start.7 = (bf16[512,1280]{1,0:T(8,128)(2,1)}, bf16[512,1280]{1,0:T(8,128)(2,1)}, u32[]{:S(2)}, u32[]{:S(2)}) collective-permute-start(bf16[512,1280]{1,0:T(8,128)(2,1)} %fusion.36), channel_id=1, source_target_pairs={{1,0},{2,1},{3,2},{4,3},{5,4},{6,5},{7,6},{9,8},{10,9},{11,10},{12... | collective-permute-start | bytes 3932168 | tf_op jit(solution)/shard_map/ppermute | solution.py:21
  750.9 283.1 %all-reduce.14.cloned.1.call-start = ((), (), s32[]{:S(2)}) async-start(), calls=%async_computation.12 | async-start | bytes 4915200 | tf_op jit(solution)/shard_map/psum | solution.py:248
  818.6 155.7 %copy-start.11 = (f32[512,1280]{1,0:T(8,128)S(1)}, f32[512,1280]{1,0:T(8,128)}, u32[]{:S(2)}) copy-start(f32[512,1280]{1,0:T(8,128)} %copy-done.10) | copy-start | bytes 7864324
  (58 other events, 1034.4 us)
Sparse Core Ops, SparseCore 0:
  10.2 145.8 all-gather.4
  158.3 79.1 all-gather.6
  239.7 88.2 all-gather.8
  330.1 78.6 all-gather.10
  436.7 127.8 reduce-scatter.8
  568.5 81.3 reduce-scatter.6
  653.5 148.5 reduce-scatter.10
  806.1 168.1 reduce-scatter.4
  977.1 56.8 all-reduce.13
where the time goes:
time: 1050 us
  waiting for transfers between devices  434 us (41%)
  matrix products  208 us (20%)
  blocking collectives  150 us (14%)
  other arithmetic  101 us (10%)
  starting transfers between devices  76.2 us (7%)
  local copies, waits for them, and re-layouts  61.7 us (6%)
  between operations  16.2 us (2%)
    ppermute x10, waiting for transfers between devices, from_behind(): lax.ppermute(value, axis, [(source, source + steps) for source in range(f...  184 us
    all_gather x1, waiting for transfers between devices, body(): lax.all_gather(qkv_weight, 'shard', axis=0, tiled=True)  101 us
    reduce_scatter x1, waiting for transfers between devices, body(): lax.psum_scatter(qkv_grad.astype(jnp.bfloat16), 'shard', scatter_dimensio...  96.5 us
    unnamed x2, blocking collectives  78.8 us
    ppermute x10, starting transfers between devices, from_behind(): lax.ppermute(value, axis, [(source, source + steps) for source in range(f...  75.1 us
    psum x1, blocking collectives, body(): scale_grad = lax.psum(scale_term, ('rep', 'shard'))  65.2 us
    psum x1, waiting for transfers between devices, body(): lax.psum(owned[1].astype(jnp.bfloat16), 'rep').astype(jnp.float32)  50.5 us
    convert_element_type x2, other arithmetic, body(): grad_scores = (probs * (grad_probs - inner_sum)).astype(bf16)  38.2 us
  transfers between devices with their start and end apart: 19, of which 10 were waited for; matrix products, arithmetic and copies ran while one was open for 33% of the time, Pallas kernels for 0%

commit v1 on v0

v1 whole, which is shorter than its diff:
```python
import functools
import math

import jax
import jax.numpy as jnp
from jax import lax
from jax.experimental import pallas as pl
from jax.experimental.pallas import tpu as pltpu
from jax.sharding import PartitionSpec as P

HEAD = 80
WINDOW = 1024
EPS = 1e-06
LOG2E = 1.442695041
LN2 = math.log(2.0)
MASKED = -1e30
TILE = 256
MESH = pl.DeviceIdType.MESH
F32 = jnp.float32
BF16 = jnp.bfloat16
VMEM_LIMIT = 62 * 2**20
ANY = pl.BlockSpec(memory_space=pl.ANY)
VM = pl.BlockSpec(memory_space=pltpu.VMEM)


def mul(a, b, left=1, right=0):
    return lax.dot_general(a, b, (((left,), (right,)), ((), ())), preferred_element_type=F32)


def at(start, size, unit):
    return pl.ds(pl.multiple_of(start, unit), size)


def bit_of(index, bit):
    return lax.rem(lax.div(index, 1 << bit), 2)


def flip(index, mask):
    out = index
    bit = 0
    while mask >> bit:
        if (mask >> bit) & 1:
            out = out + (1 - 2 * bit_of(index, bit)) * (1 << bit)
        bit += 1
    return out


def span(bits):
    masks = [0]
    for bit in bits:
        masks = masks + [mask | (1 << bit) for mask in masks]
    return masks


def stage_orders(bits):
    rest = list(range(2, bits))
    return (["x", 0, 1] + rest, [0, 1, "x"] + rest, [1, "x", 0] + rest)


def greet(count):
    rep, shard = lax.axis_index("rep"), lax.axis_index("shard")
    barrier = pltpu.get_barrier_semaphore()
    for step in range(1, count):
        other = lax.rem(shard + step, count)
        pl.semaphore_signal(barrier, inc=1, device_id={"rep": rep, "shard": other}, device_id_type=MESH)
    for mask in (1, 2):
        pl.semaphore_signal(barrier, inc=1, device_id={"rep": flip(rep, mask), "shard": shard}, device_id_type=MESH)
    pl.semaphore_wait(barrier, count + 1)


class Sems:
    def __init__(self, send, recv):
        self.send, self.recv, self.used = send, recv, 0

    def slot(self):
        self.used += 1
        return self.used - 1

    def remote(self, src, dst, rep, shard, slot=None):
        slot = self.slot() if slot is None else slot
        return pltpu.make_async_remote_copy(
            src_ref=src,
            dst_ref=dst,
            send_sem=self.send.at[slot],
            recv_sem=self.recv.at[slot],
            device_id={"rep": rep, "shard": shard},
            device_id_type=MESH,
        )


class Doubling:
    def __init__(self, sems, count, rows, parts):
        self.sems, self.rows, self.half, self.parts = sems, rows, rows // 2, parts
        bits = count.bit_length() - 1
        self.stages = bits + 1
        self.plan = []
        for order in stage_orders(bits):
            have, whole, stages = [], False, []
            for what in order[::-1]:
                masks = span(have)[1:] if what == "x" else span(have)
                stages.append([(what, mask, whole, sems.slot(), sems.slot()) for mask in masks])
                if what == "x":
                    whole = True
                else:
                    have.append(what)
            self.plan.append(stages)

    def copy(self, part, step):
        what, mask, whole, slot, _ = step
        rep, shard = lax.axis_index("rep"), lax.axis_index("shard")
        core, cross = lax.rem(rep, 2), lax.div(rep, 2)
        src, dst, first, cols = self.parts[part]
        across = at(first + core * cols, cols, 128)
        shift, size = (0, self.rows) if whole else (cross * self.half, self.half)
        row = flip(shard, mask) * self.rows + shift
        to = dst.at[at(row, size, 16), across]
        here = src.at[at(shift, size, 16), across] if mask == 0 else to
        if what == "x":
            return self.sems.remote(here, to, flip(rep, 2), shard, slot)
        return self.sems.remote(here, to, rep, flip(shard, 1 << what), slot)

    def ahead(self, part, step):
        what, mask, whole, _, slot = step
        rep, shard = lax.axis_index("rep"), lax.axis_index("shard")
        core, cross = lax.rem(rep, 2), lax.div(rep, 2)
        _, dst, first, cols = self.parts[part]
        if what == "x":
            row, size = flip(shard, mask) * self.rows + (1 - cross) * self.half, self.half
        else:
            shift, size = (0, self.rows) if whole else (cross * self.half, self.half)
            row = flip(shard, mask | (1 << what)) * self.rows + shift
        spot = dst.at[at(row, size, 16), at(first + core * cols, cols, 128)]
        return self.sems.remote(spot, spot, flip(rep, 1), shard, slot)

    def send(self, stage):
        for part in range(3):
            for step in self.plan[part][stage]:
                self.copy(part, step).start()

    def settle(self, stage):
        for part in range(3):
            for step in self.plan[part][stage]:
                self.copy(part, step).wait_recv()
                self.ahead(part, step).start()

    def move(self, stage):
        for part in range(3):
            for step in self.plan[part][stage]:
                self.copy(part, step).wait_recv()
            for step in self.plan[part][stage + 1]:
                self.copy(part, step).start()
            for step in self.plan[part][stage]:
                self.ahead(part, step).start()

    def finish(self):
        for part in range(3):
            for stage in self.plan[part]:
                for step in stage:
                    self.ahead(part, step).wait_recv()

    def drain(self):
        for part in range(3):
            for stage in self.plan[part]:
                for step in stage:
                    self.copy(part, step).wait_send()
                    self.ahead(part, step).wait_send()


class Gathered:
    stages = 1

    def send(self, stage):
        pass

    settle = move = send

    def finish(self):
        pass

    drain = finish


def forward_kernel(count, *refs):
    (tokens, earlier, segs, vec, factor, w_qkv, w_out, w_up, w_down) = refs[:9]
    results = refs[9:26]
    alone = earlier is not None
    (
        output_hbm, acted_t_hbm, q_t_hbm, k_t_hbm, v_t_hbm, o_t_hbm, lse, hidden_hbm,
        inner_t_hbm, upper_hbm, lower_t_hbm, rows_out, qkv_hbm, out_hbm, up_hbm, down_hbm, mask_hbm,
    ) = results
    (
        seg_ext, vec_full, qkv, out, up, down, acted, acted_t, q_t, k_t, v_t, o_t, heads, inner,
        hidden, upper, inner_t, lower_t, mask, state_low, send, recv, lsem,
    ) = refs[26:]
    rep, shard = lax.axis_index("rep"), lax.axis_index("shard")
    length, width = tokens.shape
    total = 3 * length
    rows = w_qkv.shape[0]
    tiles = width // TILE
    own = pl.ds(total - length, length)
    sems = Sems(send, recv)
    lower, output = heads, inner

    first_cols = (tiles * 3 // 5) * TILE
    rest_cols = width - first_cols
    groups = (Gathered(),) * 3 if alone else (
        Doubling(sems, count, rows, [(w_qkv, qkv, p * width, first_cols // 2) for p in range(3)]),
        Doubling(sems, count, rows, [(w_qkv, qkv, p * width + first_cols, rest_cols // 2) for p in range(3)]),
        Doubling(sems, count, rows, [(w, full, 0, width // 2) for w, full in ((w_out, out), (w_up, up), (w_down, down))]),
    )

    pairs = [(tokens, acted.at[own]), (tokens, state_low)]
    if alone:
        pairs += [(earlier, acted.at[pl.ds(0, 2 * length)]), (segs, seg_ext), (vec, vec_full)]
        pairs += [(w_qkv, qkv), (w_out, out), (w_up, up), (w_down, down)]
    else:
        mine = at(shard * rows, rows, 16)
        pairs += [(segs, seg_ext.at[2]), (vec, vec_full.at[shard])]
        pairs += [(w_qkv, qkv.at[mine]), (w_out, out.at[mine]), (w_up, up.at[mine]), (w_down, down.at[mine])]
    loads = [pltpu.make_async_copy(src, dst, lsem.at[i]) for i, (src, dst) in enumerate(pairs)]
    for copy in loads:
        copy.start()

    odd = lax.rem(shard, 2) == 1
    even = jnp.logical_not(odd)
    far_ok, far_got = shard < count - 2, shard >= 2
    buddy = flip(shard, 1)
    far_to = lax.rem(shard + 2, count)
    nchunk = 4
    part = length // nchunk
    far, near, relay, vecs = [], [], [], []
    for i in range(0 if alone else nchunk):
        here = pl.ds(i * part, part)
        far_spot, near_spot = acted.at[pl.ds(i * part, part)], acted.at[pl.ds(length + i * part, part)]
        slot = sems.slot()
        far.append(sems.remote(tokens.at[here], far_spot, rep, far_to, sems.slot()))
        near.append(sems.remote(tokens.at[here], near_spot, rep, buddy, slot))
        relay.append(sems.remote(far_spot, near_spot, rep, buddy, slot))
    if not alone:
        slot = sems.slot()
        far.append(sems.remote(segs, seg_ext.at[0], rep, far_to, sems.slot()))
        near.append(sems.remote(segs, seg_ext.at[1], rep, buddy, slot))
        relay.append(sems.remote(seg_ext.at[0], seg_ext.at[1], rep, buddy, slot))
        vecs = [
            sems.remote(vec, vec_full.at[shard], rep, lax.rem(shard + step, count), sems.slot()) for step in range(1, count)
        ]

    def far_start(*which):
        @pl.when(far_ok)
        def _():
            for i in which:
                far[i].start()

    def near_start(*which):
        @pl.when(even)
        def _():
            for i in which:
                near[i].start()

    def relay_start(*which):
        @pl.when(far_got)
        def _():
            for i in which:
                far[i].wait_recv()

        @pl.when(odd & far_got)
        def _():
            for i in which:
                relay[i].start()

    if not alone:
        greet(count)
        groups[0].send(0)
        for copy in vecs:
            copy.start()
        far_start(4, 0, 1)
        near_start(4, 0)
        groups[0].move(0)
        far_start(2)
        near_start(1)
        groups[0].move(1)
        groups[1].send(0)
        far_start(3)
        near_start(2, 3)
        relay_start(4, 0, 1)
        groups[0].move(2)
        groups[1].move(0)
        relay_start(2, 3)

    for copy in loads:
        copy.wait()
    for copy in vecs:
        copy.wait_recv()
    each = width // count
    vectors = jnp.concatenate([vec_full[i][:, :each].astype(F32) for i in range(count)], axis=1)
    rows_out[...] = vectors[:8, :]
    gain_one, gain_two = rows_out[0:1, :], rows_out[1:2, :]

    def norm_rows(i):
        sl = at(i * TILE, TILE, TILE)
        state = acted[sl, :].astype(F32)
        scale = lax.rsqrt(jnp.mean(state * state, axis=-1, keepdims=True) + EPS)
        value = (state * scale * rows_out[0:1, :]).astype(BF16)
        value = jnp.where(shard + i * TILE // length >= 2, value, jnp.zeros_like(value))
        acted[sl, :] = value
        acted_t[:, sl] = value.T

    def norm_step(i, carry):
        norm_rows(i)
        return carry

    per = length // TILE
    lax.fori_loop(2 * per, 3 * per, norm_step, 0)

    if not alone:

        @pl.when(odd)
        def _():
            for copy in near:
                copy.wait_recv()

        @pl.when(even & far_got)
        def _():
            for copy in relay:
                copy.wait_recv()

        @pl.when(odd & far_got)
        def _():
            for copy in relay:
                copy.wait_send()

    lax.fori_loop(0, 2 * per, norm_step, 0)

    mine = seg_ext[2].astype(F32)[0:1, :]
    for j in range(3):
        column = jnp.where(shard + j >= 2, seg_ext[j].astype(F32).T[:, 0:1], -1.0)
        place = lax.broadcasted_iota(jnp.int32, (length, length), 0) + j * length
        lane = lax.broadcasted_iota(jnp.int32, (length, length), 1)
        near_by = (place > lane) & (place <= lane + WINDOW)
        mask[j * length : (j + 1) * length, :] = jnp.where(near_by & (column == mine), 0.0, MASKED)

    groups[0].settle(groups[0].stages - 1)
    groups[1].move(1)
    groups[2].send(0)
    groups[0].finish()

    def project(i, carry):
        sl = at(i * TILE, TILE, TILE)
        q_t[sl, :] = (mul(acted[own, :], qkv[:, sl]) * factor[:, sl]).astype(BF16).T
        k_t[sl, :] = mul(acted[...], qkv[:, at(width + i * TILE, TILE, TILE)]).astype(BF16).T
        v_t[sl, :] = mul(acted[...], qkv[:, at(2 * width + i * TILE, TILE, TILE)]).astype(BF16).T
        return carry

    lax.fori_loop(0, first_cols // TILE, project, 0)
    groups[1].move(2)
    groups[2].move(0)

    def attend(h):
        sl = at(h * HEAD, HEAD, 16)
        scores = mul(k_t[sl, :].T, q_t[sl, :]) + mask[...]
        top = jnp.max(scores, axis=0, keepdims=True)
        probs = jnp.exp2(scores - top)
        norm = jnp.sum(probs, axis=0, keepdims=True)
        o_t[sl, :] = (mul(v_t[sl, :], probs.astype(BF16)) * (1.0 / norm)).astype(BF16)
        lse[h] = top + jnp.log2(norm)

    ready = first_cols // HEAD
    count_heads = width // HEAD

    def attend_first(h, carry):
        attend(h)

        @pl.when(h == 1)
        def _():
            groups[1].settle(groups[1].stages - 1)
            groups[2].move(1)

        @pl.when(h == 6)
        def _():
            groups[2].move(2)

        return carry

    lax.fori_loop(0, ready, attend_first, 0)
    groups[1].finish()
    lax.fori_loop(first_cols // TILE, tiles, project, 0)
    keep = [
        pltpu.make_async_copy(src, dst, lsem.at[8 + i])
        for i, (src, dst) in enumerate(((qkv, qkv_hbm), (acted_t, acted_t_hbm), (q_t, q_t_hbm), (k_t, k_t_hbm), (v_t, v_t_hbm), (mask, mask_hbm)))
    ]
    for copy in keep:
        copy.start()

    def attend_rest(h, carry):
        attend(h)

        @pl.when(h == count_heads - 3)
        def _():
            groups[2].settle(groups[2].stages - 1)

        return carry

    lax.fori_loop(ready, count_heads, attend_rest, 0)

    def keep_more(*pairs):
        for src, dst in pairs:
            copy = pltpu.make_async_copy(src, dst, lsem.at[8 + len(keep)])
            copy.start()
            keep.append(copy)

    keep_more((o_t, o_t_hbm))

    def turn(i, carry):
        sl = at(i * TILE, TILE, TILE)
        heads[:, sl] = o_t[sl, :].T
        return carry

    lax.fori_loop(0, tiles, turn, 0)
    groups[2].finish()
    keep_more((out, out_hbm), (up, up_hbm), (down, down_hbm))

    def out_step(i, carry):
        sl = at(i * TILE, TILE, TILE)
        hidden[:, sl] = state_low[:, sl].astype(F32) + mul(heads[...], out[:, sl])
        return carry

    lax.fori_loop(0, tiles, out_step, 0)
    keep_more((hidden, hidden_hbm))

    def norm_two(i, carry):
        sl = at(i * TILE, TILE, TILE)
        value = hidden[sl, :]
        scale = lax.rsqrt(jnp.mean(value * value, axis=-1, keepdims=True) + EPS)
        normed = (value * scale * rows_out[1:2, :]).astype(BF16)
        inner[sl, :] = normed
        inner_t[:, sl] = normed.T
        return carry

    lax.fori_loop(0, length // TILE, norm_two, 0)
    keep_more((inner_t, inner_t_hbm))

    def up_step(i, carry):
        sl = at(i * TILE, TILE, TILE)
        value = mul(inner[...], up[:, sl]) + rows_out[2:3, sl]
        upper[:, sl] = value
        act = (value / (1.0 + jnp.exp(-value))).astype(BF16)
        lower[:, sl] = act
        lower_t[sl, :] = act.T
        return carry

    lax.fori_loop(0, tiles, up_step, 0)
    keep_more((upper, upper_hbm), (lower_t, lower_t_hbm))

    def down_step(i, carry):
        sl = at(i * TILE, TILE, TILE)
        output[:, sl] = (hidden[:, sl] + (mul(lower[...], down[:, sl]) + rows_out[3:4, sl])).astype(BF16)
        return carry

    lax.fori_loop(0, tiles, down_step, 0)
    keep_more((output, output_hbm))

    if not alone:

        @pl.when(far_ok)
        def _():
            for copy in far:
                copy.wait_send()

        @pl.when(even)
        def _():
            for copy in near:
                copy.wait_send()

    for copy in vecs:
        copy.wait_send()
    for group in groups:
        group.drain()
    for copy in keep:
        copy.wait()


def forward(count, tokens, earlier, segs, vec, factor, w_qkv, w_out, w_up, w_down):
    length, width = tokens.shape
    total = 3 * length
    heads = width // HEAD
    inputs = [x for x in (tokens, earlier, segs, vec, factor, w_qkv, w_out, w_up, w_down) if x is not None]
    if earlier is None:
        params = pltpu.CompilerParams(collective_id=0, has_side_effects=True, vmem_limit_bytes=VMEM_LIMIT)
    else:
        params = pltpu.CompilerParams(vmem_limit_bytes=VMEM_LIMIT)
    shape = jax.ShapeDtypeStruct
    outs = (
        shape((length, width), BF16),
        shape((width, total), BF16),
        shape((width, length), BF16),
        shape((width, total), BF16),
        shape((width, total), BF16),
        shape((width, length), BF16),
        shape((heads, 1, length), F32),
        shape((length, width), F32),
        shape((width, length), BF16),
        shape((length, width), F32),
        shape((width, length), BF16),
        shape((8, width), F32),
        shape((width, 3 * width), BF16),
        shape((width, width), BF16),
        shape((width, width), BF16),
        shape((width, width), BF16),
        shape((total, length), F32),
    )
    specs = [ANY] * 17
    specs[6] = specs[11] = VM
    buffer = pltpu.VMEM
    return pl.pallas_call(
        functools.partial(forward_kernel, count) if earlier is not None else lambda *refs: forward_kernel(count, refs[0], None, *refs[1:]),
        name="forward_layer",
        out_shape=outs,
        in_specs=[ANY] * (len(inputs) - 5) + [VM] + [ANY] * 4,
        out_specs=tuple(specs),
        scratch_shapes=[
            buffer((3,) + segs.shape[-2:], jnp.int32),
            buffer((count,) + vec.shape[-2:], BF16),
            buffer((width, 3 * width), BF16),
            buffer((width, width), BF16),
            buffer((width, width), BF16),
            buffer((width, width), BF16),
            buffer((total, width), BF16),
            buffer((width, total), BF16),
            buffer((width, length), BF16),
            buffer((width, total), BF16),
            buffer((width, total), BF16),
            buffer((width, length), BF16),
            buffer((length, width), BF16),
            buffer((length, width), BF16),
            buffer((length, width), F32),
            buffer((length, width), F32),
            buffer((width, length), BF16),
            buffer((width, length), BF16),
            buffer((total, length), F32),
            buffer((length, width), BF16),
            pltpu.SemaphoreType.DMA((256,)),
            pltpu.SemaphoreType.DMA((256,)),
            pltpu.SemaphoreType.DMA((32,)),
        ],
        compiler_params=params,
    )(*inputs)


def backward_kernel(*refs):
    (cot, mask, gain_two, hidden, inner_t, upper, lower_t, o_t, q_t, k_t, v_t, lse, out, up, down) = refs[:15]
    (down_grad, up_grad, out_grad, grad_hidden, dq_t, dk_t, dv_t, rows_out) = refs[15:23]
    grad_upper, grad_attn, do_t = refs[23:]
    length, width = cot.shape
    tiles = width // TILE
    rows_out[...] = jnp.zeros_like(rows_out)

    def down_step(i, carry):
        sl = at(i * TILE, TILE, TILE)
        down_grad[:, sl] = mul(lower_t[...], cot[:, sl]).astype(BF16)
        grad_lower = mul(cot[...], down[sl, :], 1, 1)
        value = upper[:, sl]
        gate = 1.0 / (1.0 + jnp.exp(-value))
        grad = (grad_lower * (gate + value * gate * (1.0 - gate))).astype(BF16)
        grad_upper[:, sl] = grad
        rows_out[2:3, sl] = jnp.sum(grad.astype(F32), axis=0, keepdims=True)
        rows_out[3:4, sl] = jnp.sum(cot[:, sl].astype(F32), axis=0, keepdims=True)
        return carry

    lax.fori_loop(0, tiles, down_step, 0)

    def up_step(i, carry):
        sl = at(i * TILE, TILE, TILE)
        up_grad[:, sl] = mul(inner_t[...], grad_upper[:, sl]).astype(BF16)
        grad_hidden[:, sl] = mul(grad_upper[...], up[sl, :], 1, 1)
        return carry

    lax.fori_loop(0, tiles, up_step, 0)

    def norm_step(i, carry):
        sl = at(i * TILE, TILE, TILE)
        value = hidden[sl, :]
        scale = lax.rsqrt(jnp.mean(value * value, axis=-1, keepdims=True) + EPS)
        normed = value * scale
        grad = grad_hidden[sl, :]
        rows_out[1:2, :] += jnp.sum(grad * normed, axis=0, keepdims=True)
        weighted = grad * gain_two[...]
        along = jnp.mean(weighted * normed, axis=-1, keepdims=True)
        total = cot[sl, :].astype(F32) + scale * (weighted - normed * along)
        grad_hidden[sl, :] = total
        grad_attn[sl, :] = total.astype(BF16)
        return carry

    lax.fori_loop(0, length // TILE, norm_step, 0)

    def out_step(i, carry):
        sl = at(i * TILE, TILE, TILE)
        out_grad[:, sl] = mul(o_t[...], grad_attn[:, sl]).astype(BF16)
        do_t[sl, :] = mul(grad_attn[...], out[sl, :], 1, 1).astype(BF16).T
        return carry

    lax.fori_loop(0, tiles, out_step, 0)

    def attend(h, carry):
        sl = at(h * HEAD, HEAD, 16)
        query, key, grad = q_t[sl, :], k_t[sl, :], do_t[sl, :]
        probs = jnp.exp2(mul(key.T, query) + mask[...] - lse[h])
        delta = jnp.sum(o_t[sl, :].astype(F32) * grad.astype(F32), axis=0, keepdims=True)
        scores = (probs * (mul(v_t[sl, :].T, grad) - delta)).astype(BF16)
        dv_t[sl, :] = mul(grad, probs.astype(BF16), 1, 1).astype(BF16)
        dk_t[sl, :] = (mul(query, scores, 1, 1) * LN2).astype(BF16)
        dq_t[sl, :] = mul(key, scores)
        return carry

    lax.fori_loop(0, width // HEAD, attend, 0)


def backward(cot, mask, gain_two, hidden, inner_t, upper, lower_t, o_t, q_t, k_t, v_t, lse, out, up, down):
    length, width = cot.shape
    total = k_t.shape[1]
    shape = jax.ShapeDtypeStruct
    return pl.pallas_call(
        backward_kernel,
        name="backward_layer",
        out_shape=(
            shape((width, width), BF16),
            shape((width, width), BF16),
            shape((width, width), BF16),
            shape((length, width), F32),
            shape((width, length), F32),
            shape((width, total), BF16),
            shape((width, total), BF16),
            shape((8, width), F32),
        ),
        in_specs=[VM] * 15,
        out_specs=(VM,) * 8,
        scratch_shapes=[
            pltpu.VMEM((length, width), BF16),
            pltpu.VMEM((length, width), BF16),
            pltpu.VMEM((width, length), BF16),
        ],
        compiler_params=pltpu.CompilerParams(vmem_limit_bytes=VMEM_LIMIT),
    )(cot, mask, gain_two, hidden, inner_t, upper, lower_t, o_t, q_t, k_t, v_t, lse, out, up, down)


def project_back_kernel(*refs):
    (dq_t, dk_t, dv_t, q_t, acted_t, qkv, factor, gain_one) = refs[:8]
    (qkv_grad, grad_acted, gain_row, scale_col) = refs[8:12]
    (dq_low,) = refs[12:]
    width, total = acted_t.shape
    length = dq_t.shape[1]
    tiles = width // TILE
    own = pl.ds(total - length, length)
    scale_col[...] = jnp.zeros_like(scale_col)

    def scale_step(h, carry):
        sl = at(h * HEAD, HEAD, 16)
        grad = dq_t[sl, :]
        scale_col[...] += jnp.sum(grad * q_t[sl, :].astype(F32), axis=1, keepdims=True)
        dq_low[sl, :] = (grad * factor[sl, :]).astype(BF16)
        return carry

    lax.fori_loop(0, width // HEAD, scale_step, 0)

    def weight_step(i, carry):
        sl = at(i * TILE, TILE, TILE)
        qkv_grad[:, sl] = mul(acted_t[:, own], dq_low[sl, :], 1, 1).astype(BF16)
        qkv_grad[:, at(width + i * TILE, TILE, TILE)] = mul(acted_t[...], dk_t[sl, :], 1, 1).astype(BF16)
        qkv_grad[:, at(2 * width + i * TILE, TILE, TILE)] = mul(acted_t[...], dv_t[sl, :], 1, 1).astype(BF16)
        return carry

    lax.fori_loop(0, tiles, weight_step, 0)

    def state_step(i, carry):
        sl = at(i * TILE, TILE, TILE)
        wide = mul(qkv[sl, width : 2 * width], dk_t[...]) + mul(qkv[sl, 2 * width : 3 * width], dv_t[...])
        mine = wide[:, total - length :] + mul(qkv[sl, :width], dq_low[...])
        both = jnp.concatenate([wide[:, : total - length], mine], axis=1)
        low = both.astype(BF16)
        sums = jnp.sum(both * acted_t[sl, :].astype(F32), axis=1, keepdims=True)
        gain_row[sl, :] = sums / gain_one[sl, :]
        for j in range(total // length):
            grad_acted[j, :, sl] = low[:, j * length : (j + 1) * length].T
        return carry

    lax.fori_loop(0, tiles, state_step, 0)


def project_back(dq_t, dk_t, dv_t, q_t, acted_t, qkv, factor, gain_one):
    width, total = acted_t.shape
    length = dq_t.shape[1]
    shape = jax.ShapeDtypeStruct
    return pl.pallas_call(
        project_back_kernel,
        name="backward_projection",
        out_shape=(
            shape((width, 3 * width), BF16),
            shape((total // length, length, width), BF16),
            shape((width, 1), F32),
            shape((HEAD, 1), F32),
        ),
        in_specs=[VM] * 8,
        out_specs=(VM,) * 4,
        scratch_shapes=[pltpu.VMEM((width, length), BF16)],
        compiler_params=pltpu.CompilerParams(vmem_limit_bytes=VMEM_LIMIT),
    )(dq_t, dk_t, dv_t, q_t, acted_t, qkv, factor, gain_one)


def reduce_kernel(count, *refs):
    (qkv_grad, out_grad, up_grad, down_grad, grad_acted, small) = refs[:6]
    (qkv_own, out_own, up_own, down_own, acted_own, small_sum) = refs[6:12]
    (acc, core_in, stage_in, result, far_in, near_in, far_out, small_now, small_in, send, recv, lsem) = refs[12:]
    rep, shard = lax.axis_index("rep"), lax.axis_index("shard")
    core, cross = lax.rem(rep, 2), lax.div(rep, 2)
    bits = count.bit_length() - 1
    width = out_grad.shape[1]
    rows = width // count
    half = rows // 2
    cols = width // 2
    length = grad_acted.shape[1]
    sems = Sems(send, recv)

    def block(weight, part_no, core_no):
        if weight == 0:
            return (out_grad, up_grad, down_grad)[part_no].at[:, at(core_no * cols, cols, 128)]
        return qkv_grad.at[:, at(part_no * width + core_no * cols, cols, 128)]

    loads = []
    for weight in (0, 1):
        for part_no in range(3):
            slot = 3 * weight + part_no
            copy = pltpu.make_async_copy(block(weight, part_no, core), acc.at[slot], lsem.at[slot])
            copy.start()
            loads.append(copy)
    fetch = pltpu.make_async_copy(small, small_now.at[0], lsem.at[6])
    fetch.start()
    mine = pltpu.make_async_copy(grad_acted.at[2], acted_own.at[0], lsem.at[7])
    mine.start()
    greet(count)

    pending = []
    exchange = []
    for weight in (0, 1):
        for part_no in range(3):
            copy = sems.remote(block(weight, part_no, 1 - core), core_in.at[3 * weight + part_no], flip(rep, 1), shard)
            copy.start()
            exchange.append(copy)
    pending += exchange

    odd = lax.rem(shard, 2) == 1
    far_ok, far_got = shard >= 2, shard < count - 2
    buddy = flip(shard, 1)
    far_to = lax.rem(shard + count - 2, count)
    give = sems.remote(grad_acted.at[1], near_in, rep, buddy)
    far = sems.remote(far_out, acted_own.at[1], rep, far_to)
    load_far = pltpu.make_async_copy(grad_acted.at[0], far_in, lsem.at[8])
    load_far.start()

    @pl.when(odd | far_ok)
    def _():
        give.start()

    def small_stage(number):
        partner = ("core", "x") + tuple(range(bits))
        what = partner[number]
        to_rep = flip(rep, 1) if what == "core" else flip(rep, 2) if what == "x" else rep
        to_shard = flip(shard, 1 << what) if isinstance(what, int) else shard
        return sems.remote(small_now.at[number], small_in.at[number], to_rep, to_shard)

    fetch.wait()
    small_copy = small_stage(0)
    small_copy.start()
    small_number = 0

    def add_rows(slot, row, size, other):
        sl = at(row, size, 16)
        acc[slot, sl, :] = (acc[slot, sl, :].astype(F32) + other.astype(F32)).astype(BF16)

    def add_core(slot):
        def step(i, carry):
            sl = at(i * TILE, TILE, TILE)
            acc[slot, sl, :] = (acc[slot, sl, :].astype(F32) + core_in[slot, sl, :].astype(F32)).astype(BF16)
            return carry

        lax.fori_loop(0, width // TILE, step, 0)

    orders = stage_orders(bits)
    for weight in (0, 1):
        left = [list(range(bits)) for _ in range(3)]
        done_x = [False] * 3
        arriving = [[] for _ in range(3)]
        base = [0] * 3
        for stage in range(bits + 2):
            for part_no in range(3):
                slot = 3 * weight + part_no
                if stage == 0:
                    loads[slot].wait()
                    exchange[slot].wait_recv()
                    add_core(slot)
                for copy, row, size, spot in arriving[part_no]:
                    copy.wait_recv()
                    add_rows(slot, row, size, stage_in[slot, pl.ds(spot, size), :])
                arriving[part_no] = []
                if stage > bits:
                    continue
                what = orders[part_no][stage]
                if what == "x":
                    for mask in span(left[part_no]):
                        row = flip(shard, mask) * rows
                        spot = base[part_no]
                        copy = sems.remote(
                            acc.at[slot, at(row + (1 - cross) * half, half, 16)],
                            stage_in.at[slot, pl.ds(spot, half)],
                            flip(rep, 2),
                            shard,
                        )
                        copy.start()
                        pending.append(copy)
                        arriving[part_no].append((copy, row + cross * half, half, spot))
                        base[part_no] += half
                    done_x[part_no] = True
                else:
                    left[part_no].remove(what)
                    shift, size = (cross * half, half) if done_x[part_no] else (0, rows)
                    for mask in span(left[part_no]):
                        spot = base[part_no]
                        copy = sems.remote(
                            acc.at[slot, at(flip(shard, mask | (1 << what)) * rows + shift, size, 16)],
                            stage_in.at[slot, pl.ds(spot, size)],
                            rep,
                            flip(shard, 1 << what),
                        )
                        copy.start()
                        pending.append(copy)
                        arriving[part_no].append((copy, flip(shard, mask) * rows + shift, size, spot))
                        base[part_no] += size
            if small_number < bits + 2:
                small_copy.wait()
                small_now[small_number + 1] = small_now[small_number] + small_in[small_number]
                small_number += 1
                if small_number < bits + 2:
                    small_copy = small_stage(small_number)
                    small_copy.start()
            if weight == 0 and stage == 1:

                @pl.when(jnp.logical_not(odd) | far_ok)
                def _():
                    give.wait_recv()

                load_far.wait()

                def far_step(i, carry):
                    sl = at(i * 128, 128, 128)
                    value = far_in[sl, :].astype(F32)
                    value = jnp.where(odd, value + near_in[sl, :].astype(F32), value)
                    far_out[sl, :] = value.astype(BF16)
                    return carry

                @pl.when(far_ok)
                def _():
                    lax.fori_loop(0, length // 128, far_step, 0)
                    far.start()

        crossing = []
        for part_no in range(3):
            slot = 3 * weight + part_no
            src = acc.at[slot, at(shard * rows + cross * half, half, 16)]
            copy = sems.remote(src, result.at[slot, core, at(cross * half, half, 16)], flip(rep, 2), shard)
            copy.start()
            crossing.append(copy)
            result[slot, core, at(cross * half, half, 16), :] = acc[slot, at(shard * rows + cross * half, half, 16), :]
        pending += crossing
        sharing = []
        for part_no in range(3):
            slot = 3 * weight + part_no
            crossing[part_no].wait_recv()
            copy = sems.remote(result.at[slot, core], result.at[slot, core], flip(rep, 1), shard)
            copy.start()
            sharing.append(copy)
        pending += sharing
        for part_no in range(3):
            slot = 3 * weight + part_no
            sharing[part_no].wait_recv()
            for side in range(2):
                value = result[slot, side].astype(F32)
                if weight == 0:
                    (out_own, up_own, down_own)[part_no][:, side * cols : (side + 1) * cols] = value
                else:
                    first = part_no * width + side * cols
                    qkv_own[:, first : first + cols] = value

    small_sum[...] = small_now[bits + 2]

    @pl.when(odd | far_ok)
    def _():
        give.wait_send()

    @pl.when(far_ok)
    def _():
        far.wait_send()

    @pl.when(far_got)
    def _():
        far.wait_recv()

    mine.wait()
    keep_near = pltpu.make_async_copy(near_in, acted_own.at[2], lsem.at[9])

    @pl.when(jnp.logical_not(odd))
    def _():
        keep_near.start()
        keep_near.wait()

    for copy in pending:
        copy.wait_send()


def reduce(count, qkv_grad, out_grad, up_grad, down_grad, grad_acted, small):
    width = out_grad.shape[1]
    rows = width // count
    length = grad_acted.shape[1]
    bits = count.bit_length() - 1
    shape = jax.ShapeDtypeStruct
    cols = width // 2
    return pl.pallas_call(
        functools.partial(reduce_kernel, count),
        name="reduce_gradients",
        out_shape=(
            shape((rows, 3 * width), F32),
            shape((rows, width), F32),
            shape((rows, width), F32),
            shape((rows, width), F32),
            shape((3, length, width), BF16),
            shape(small.shape, F32),
        ),
        in_specs=[ANY] * 6,
        out_specs=(VM, VM, VM, VM, ANY, VM),
        scratch_shapes=[
            pltpu.VMEM((6, width, cols), BF16),
            pltpu.VMEM((6, width, cols), BF16),
            pltpu.VMEM((6, width, cols), BF16),
            pltpu.VMEM((6, 2, rows, cols), BF16),
            pltpu.VMEM((length, width), BF16),
            pltpu.VMEM((length, width), BF16),
            pltpu.VMEM((length, width), BF16),
            pltpu.VMEM((bits + 3,) + small.shape, F32),
            pltpu.VMEM((bits + 2,) + small.shape, F32),
            pltpu.SemaphoreType.DMA((256,)),
            pltpu.SemaphoreType.DMA((256,)),
            pltpu.SemaphoreType.DMA((16,)),
        ],
        compiler_params=pltpu.CompilerParams(collective_id=1, has_side_effects=True, vmem_limit_bytes=VMEM_LIMIT),
    )(qkv_grad, out_grad, up_grad, down_grad, grad_acted, small)


def shifted(value, steps):
    count = lax.axis_size("shard")
    first, last = (max(0, -steps), min(count, count - steps))
    return lax.ppermute(value, "shard", [(source, source + steps) for source in range(first, last)])


def gather_plain(tokens, segs, vec, *weights):
    whole = tuple(lax.all_gather(weight, "shard", axis=0, tiled=True) for weight in weights)
    earlier = jnp.concatenate([shifted(tokens, 2), shifted(tokens, 1)])
    seg_ext = jnp.stack([shifted(segs, 2), shifted(segs, 1), segs])
    return (earlier, seg_ext, lax.all_gather(vec, "shard", axis=0)) + whole


def reduce_plain(qkv_grad, out_grad, up_grad, down_grad, grad_acted, small):
    owned = []
    for grad in (qkv_grad, out_grad, up_grad, down_grad):
        part = lax.psum_scatter(grad, "shard", scatter_dimension=0, tiled=True)
        owned.append(lax.psum(part, "rep").astype(F32))
    parts = jnp.stack([grad_acted[2], shifted(grad_acted[0], -2), shifted(grad_acted[1], -1)])
    return (*owned, parts, lax.psum(small, ("rep", "shard")))


def body(
    tokens,
    segments,
    cotangent,
    gain_one,
    qkv_weight,
    query_scale,
    out_weight,
    gain_two,
    up_weight,
    up_bias,
    down_weight,
    down_bias,
):
    count = lax.axis_size("shard")
    shard = lax.axis_index("shard")
    length, width = tokens.shape[1:]
    rows = qkv_weight.shape[0]
    heads = width // HEAD

    vec = jnp.stack([gain_one, gain_two, up_bias, down_bias])
    vec = jnp.pad(vec, ((0, 12), (0, -rows % 128)))
    segs = jnp.broadcast_to(segments, (8, length))
    whole_tiles = rows % 32 == 0 and count >= 4 and count & (count - 1) == 0 and lax.axis_size("rep") == 4
    reduce_all = functools.partial(reduce, count) if whole_tiles else reduce_plain
    factor = LOG2E / math.sqrt(HEAD) * jax.nn.softplus(query_scale)
    factor_row = jnp.tile(factor, heads)[None]
    weights = (qkv_weight, out_weight, up_weight, down_weight)
    earlier = None
    if not whole_tiles:
        earlier, segs, vec, *weights = gather_plain(tokens[0], segs, vec, *weights)
    output, acted_t, q_t, k_t, v_t, o_t, lse, hidden, inner_t, upper, lower_t, rows_in, qkv, out, up, down, mask = forward(
        count, tokens[0], earlier, segs, vec, factor_row * (1.0 / LN2), *weights
    )
    gain_one_row, gain_two_row = rows_in[0:1], rows_in[1:2]
    down_grad, up_grad, out_grad, grad_hidden, dq_t, dk_t, dv_t, rows_out = backward(
        cotangent[0], mask, gain_two_row, hidden, inner_t, upper, lower_t, o_t, q_t, k_t, v_t, lse, out, up, down
    )
    qkv_grad, grad_acted, gain_col, scale_col = project_back(
        dq_t, dk_t, dv_t, q_t, acted_t, qkv, factor_row.reshape(width, 1), gain_one_row.reshape(width, 1)
    )
    scale_row = jnp.pad(scale_col[:, 0], (0, width - HEAD))
    small_rows = jnp.concatenate([gain_col.reshape(1, width), rows_out[1:4], scale_row[None], rows_out[5:]], 0)
    qkv_own, out_own, up_own, down_own, acted_parts, small_sum = reduce_all(
        qkv_grad, out_grad, up_grad, down_grad, grad_acted, small_rows
    )
    far_got = shard < count - 2
    near_got = (lax.rem(shard, 2) == 0) if whole_tiles else (shard < count - 1)
    total = acted_parts[0].astype(F32)
    total += jnp.where(far_got, acted_parts[1], 0).astype(F32)
    total += jnp.where(near_got, acted_parts[2], 0).astype(F32)
    state = tokens[0].astype(F32)
    inverse = lax.rsqrt(jnp.mean(state * state, axis=-1, keepdims=True) + EPS)
    normed = state * inverse
    weighted = total * gain_one_row
    along = jnp.mean(weighted * normed, axis=-1, keepdims=True)
    input_grad = (grad_hidden + inverse * (weighted - normed * along)).astype(BF16)

    mine = lax.dynamic_slice_in_dim(small_sum[:4], shard * rows, rows, 1)
    scale_grad = (
        small_sum[4, :HEAD]
        * LN2
        / factor
        * (LOG2E / math.sqrt(HEAD))
        * jax.nn.sigmoid(query_scale)
    )
    return (
        output[None],
        input_grad[None],
        mine[0],
        qkv_own,
        scale_grad,
        out_own,
        mine[1],
        up_own,
        mine[2],
        down_own,
        mine[3],
    )


def solution(mesh):
    return jax.shard_map(
        body,
        mesh=mesh,
        in_specs=(
            P("rep", "shard", None),
            P("rep", "shard"),
            P("rep", "shard", None),
            P("shard"),
            P("shard", None),
            P(),
            P("shard", None),
            P("shard"),
            P("shard", None),
            P("shard"),
            P("shard", None),
            P("shard"),
        ),
        out_specs=(
            P("rep", "shard", None),
            P("rep", "shard", None),
            P("shard"),
            P("shard", None),
            P(),
            P("shard", None),
            P("shard"),
            P("shard", None),
            P("shard"),
            P("shard", None),
            P("shard"),
        ),
        check_vma=False,
    )
```

time: 1050 us -> 466 us (0.44)
  Pallas kernels: 0 us -> 435 us
  waiting for transfers between devices: 434 us -> 0 us
  matrix products: 208 us -> 0 us
  blocking collectives: 150 us -> 0 us
  other arithmetic: 101 us -> 10.8 us
  starting transfers between devices: 76.2 us -> 0 us
  local copies, waits for them, and re-layouts: 61.7 us -> 16.2 us
  between operations: 16.2 us -> 0.78 us
    pallas_call x0 -> x4, Pallas kernels: none -> 435 us  [the longest x1 182 us: reduce(): pl.pallas_call(functools.partial(reduce_kernel, count), name='reduce_grad...]
    dot_general x24 -> x0, matrix products: 208 us -> none  [the longest x2 32.8 us: body(): jnp.einsum('qhd,khd->hqk', shaped_grad, shaped_value, preferred_element_t...]
    ppermute x10 -> x0, waiting for transfers between devices: 184 us -> none  [from_behind(): lax.ppermute(value, axis, [(source, source + steps) for source in range(f...]
    all_gather x4 -> x0, waiting for transfers between devices: 101 us -> none  [the longest x1 101 us: body(): lax.all_gather(qkv_weight, 'shard', axis=0, tiled=True)]
    reduce_scatter x4 -> x0, waiting for transfers between devices: 96.6 us -> none  [the longest x1 96.5 us: body(): lax.psum_scatter(qkv_grad.astype(jnp.bfloat16), 'shard', scatter_dimensio...]
    unnamed x2 -> x0, blocking collectives: 78.8 us -> none
    ppermute x10 -> x0, starting transfers between devices: 75.1 us -> none  [from_behind(): lax.ppermute(value, axis, [(source, source + steps) for source in range(f...]
    psum x2 -> x0, blocking collectives: 71.4 us -> none  [the longest x1 65.2 us: body(): scale_grad = lax.psum(scale_term, ('rep', 'shard'))]
  transfers between devices with their start and end apart: 19 -> 0, of which waited for: 10 -> 0; matrix products, arithmetic and copies ran while one was open for 33% -> 0% of each run, Pallas kernels for 0% -> 0%
where the time goes in v1:
time: 466 us; the launch traced here: 462 us
  Pallas kernels  435 us (93%)
  local copies, waits for them, and re-layouts  16.2 us (3%)
  other arithmetic  10.8 us (2%)
    pallas_call x1, Pallas kernels, reduce(): pl.pallas_call(functools.partial(reduce_kernel, count), name='reduce_grad...  182 us
    pallas_call x1, Pallas kernels, forward(): pl.pallas_call(functools.partial(forward_kernel, count) if earlier is not...  145 us
    pallas_call x1, Pallas kernels, backward(): pl.pallas_call(backward_kernel, name='backward_layer', out_shape=(shape((...  67.8 us
    pallas_call x1, Pallas kernels, project_back(): pl.pallas_call(project_back_kernel, name='backward_projection', out_shape...  39.9 us

profile of v1, /device:TPU:0, one launch (start us, length us, event | category | flops | bytes accessed | tf_op | source)
XLA Modules:
  0.0 462.5 jit_solution(1823301398005442076)
XLA Ops:
  0.6 0.7 broadcast_multiply_fusion.1
  1.3 0.7 mul.69.refs_3_
  2.0 1.3 broadcast_in_dim.24.refs_1_
  3.3 0.7 stack.15
  4.0 0.7 stack.16
  4.6 0.7 stack.17
  5.3 0.7 stack.18
  6.5 145.5 %forward_layer.1 = (bf16[512,1280]{1,0:T(8,128)(2,1)}, bf16[1280,1536]{1,0:T(8,128)(2,1)}, bf16[1280,512]{1,0:T(8,128)(2,1)}, bf16[1280,1536]{1,0:T(8,128)(2,1)}...) custom-call(bf16[512,1280]{1,0:T(8,128)(2,1)} %bitcast.27, ...), custom_call_target="tpu_custom_call" | custom-call | tf_op jit(solution)/shard_map/forward_layer/pallas_call | solution.py:514
  152.0 1.5 slice_bitcast_fusion
  153.5 67.8 %backward_layer.1 = (bf16[1280,1280]{1,0:T(8,128)(2,1)}, bf16[1280,1280]{1,0:T(8,128)(2,1)}, bf16[1280,1280]{1,0:T(8,128)(2,1)}, f32[512,1280]{1,0:T(8,128)}, f3...) custom-call(bf16[512,1280]{1,0:T(8,128)(2,1)} %bitcast.28, ...), custom_call_target="tpu_custom_call" | custom-call | tf_op jit(solution)/shard_map/backward_layer/pallas_call | solution.py:621
  221.2 1.1 copy.24.refs_7_
  222.4 1.1 reshape_broadcast_in_dim_tile.4.refs_6_
  223.4 39.9 %backward_projection.1 = (bf16[1280,3840]{1,0:T(8,128)(2,1)}, bf16[3,512,1280]{2,1,0:T(8,128)(2,1)}, f32[1280,1]{1,0:T(8,128)}, f32[80,1]{1,0:T(8,128)}) custom-call(f32[1280,512]{1,0:T(8,128)} %get-tuple-element.62.refs_0_, bf16[1280,1536]{1,0:T(8,128)(2,1)} %get-tuple-element.63.refs_1_, bf16[1280,1536]{1,0:T(8,128)(2,1)} %get-tuple-element.64.refs_2_, ...), custom_call_target="tpu_custom_call" | custom-call | tf_op jit(solution)/shard_map/backward_projection/pallas_call | solution.py:692
  263.3 0.9 reduce.1
  264.2 1.3 reduce
  266.3 181.5 %reduce_gradients.1 = (f32[160,3840]{1,0:T(8,128)}, f32[160,1280]{1,0:T(8,128)}, f32[160,1280]{1,0:T(8,128)}, f32[160,1280]{1,0:T(8,128)}, bf16[3,512,1280]{2,1,0:T(8,128)(2,1)}, /*index=5*/f32[8,1280]{1,0:T(8,128)}) custom-call(bf16[1280,3840]{1,0:T(8,128)(2,1)} %get-tuple-element.67.refs_0_, bf16[1280,1280]{1,0:T(8,128)(2,1)} %get-tuple-element.68.refs_1_, ...), custom_call_target="tpu_custom_call" | custom-call | tf_op jit(solution)/shard_map/reduce_gradients/pallas_call | solution.py:924
  448.2 3.4 fusion.2
  452.0 2.4 fusion.8
  454.4 0.7 fusion.22
  455.6 2.5 copy.30
  458.1 1.4 copy.31
  459.8 0.9 copy.32
  460.7 0.9 copy.33
  461.6 0.9 copy.34
  (34 shorter events, 2.9 us)
Async XLA Ops:
  223.4 42.1 %copy-start.7 = (f32[8,1280]{1,0:T(8,128)S(1)}, f32[8,1280]{1,0:T(8,128)}, u32[]{:S(2)}) copy-start(f32[8,1280]{1,0:T(8,128)} %get-tuple-element.73) | copy-start | bytes 122884
  266.3 181.5 %copy-start = (bf16[1,512,1280]{2,1,0:T(8,128)(2,1)S(1)}, bf16[1,512,1280]{2,1,0:T(8,128)(2,1)}, u32[]{:S(2)}) copy-start(bf16[1,512,1280]{2,1,0:T(8,128)(2,1)} %param.12) | copy-start | bytes 3932164
  447.8 3.8 copy-start.2
  448.2 3.8 copy-start.1
  452.0 2.4 copy-start.8
  452.0 3.1 copy-start.9
  454.4 3.7 copy-start.3
  458.1 1.7 copy-start.6
  458.1 2.6 copy-start.5
  459.8 1.8 copy-start.4
